TPU v7x, 32 devices: a whole 2x2x4 slice. The times are simulated.
32 devices in a mesh: tiles: 16 (over z, y, x), chan: 2 (over core).
Axes of the slice: x: 2, y: 2, z: 4, core: 2. Of those that a mesh axis runs over, the one named last changes fastest.
Arguments:
- ocean_state: bfloat16 [16, 22, 2, 16, 3072], P('tiles', None, 'chan'), may hold values from -24 to 24
- land_mask: int32 [16, 22], P('tiles'), may hold values from 0 to 1, as said below
- cotangent: bfloat16 [224, 2, 16, 3072], P('tiles', 'chan'), may hold values from -6 to 6
- depth_kernel: float32 [7, 7, 384], P(None, None, 'chan'), may hold values from -1.8 to 1.8
- norm_gain: float32 [384], P('chan'), may hold values from 0.5 to 1.5
- norm_shift: float32 [384], P('chan'), may hold values from -3 to 3
- weight_in: bfloat16 [384, 1536], P(None, 'chan'), may hold values from -0.3125 to 0.3125
- bias_in: float32 [1536], P('chan'), may hold values from -3 to 3
- weight_out: bfloat16 [1536, 384], P('chan'), may hold values from -0.15625 to 0.15625
- bias_out: float32 [384], P('chan'), may hold values from -3 to 3
- layer_scale: float32 [384], P('chan'), may hold values from 0.3 to 1
Outputs:
- block_out: bfloat16 [224, 2, 16, 3072], P('tiles', 'chan')
- grad_state: bfloat16 [16, 22, 2, 16, 3072], P('tiles', None, 'chan')
- grad_kernel: float32 [7, 7, 384], P(None, None, 'chan')
- grad_gain: float32 [384], P('chan')
- grad_shift: float32 [384], P('chan')
- grad_weight_in: float32 [384, 1536], P(None, 'chan')
- grad_bias_in: float32 [1536], P('chan')
- grad_weight_out: float32 [1536, 384], P('chan')
- grad_bias_out: float32 [384], P('chan')
- grad_scale: float32 [384], P('chan')
Inputs may be any that keep to these rules, and one draw needn't show every extreme that they name: `land_mask`: exactly 224 entries are 1, and some band is ocean in all its 22 slots.
All inputs are finite; a program needn't handle non-finite values.
Results may differ from a plain program's by a relative error of at most 0.014.
Values may be sent and summed in bfloat16 or wider, within the bound.
A program may use at most 128 MiB of HBM per device.

v0:
```python
import jax
import jax.numpy as jnp
from jax import lax
from jax.sharding import PartitionSpec as P

EPS = 1e-06
ROOT_TWO_PI = 0.7978845608028654
CUBIC = 0.044715
SWAP = ((0, 1), (1, 0))


def swapped(value):
    return lax.ppermute(value, "chan", SWAP)


def row_halo(field, width):
    count = lax.axis_size("tiles")
    forward = [(i, i + 1) for i in range(count - 1)]
    backward = [(target, source) for source, target in forward]
    low = lax.ppermute(field[field.shape[0] - width :], "tiles", forward)
    high = lax.ppermute(field[:width], "tiles", backward)
    return jnp.concatenate([low, field, high], axis=0)


def gelu_pair(values):
    inner_arg = ROOT_TWO_PI * (values + CUBIC * values * values * values)
    tangent = jnp.tanh(inner_arg)
    gelu_value = 0.5 * values * (1.0 + tangent)
    gelu_slope = 0.5 * (1.0 + tangent) + 0.5 * values * (1.0 - tangent * tangent) * ROOT_TWO_PI * (
        1.0 + 3.0 * CUBIC * values * values
    )
    return (gelu_value, gelu_slope)


def depthwise(padded, kernel):
    span = kernel.shape[0]
    rows, cols = (padded.shape[0] - span + 1, padded.shape[1] - span + 1)
    total = jnp.zeros((rows, cols, padded.shape[2]), jnp.float32)
    for down in range(span):
        for east in range(span):
            window = padded[down : down + rows, east : east + cols]
            total = total + window.astype(jnp.float32) * kernel[down, east]
    return total


def kernel_grads(back, framed, span):
    rows, cols = back.shape[:2]
    back_float = back.astype(jnp.float32)
    sums = []
    for down in range(span):
        for east in range(span):
            window = framed[down : down + rows, east : east + cols].astype(jnp.float32)
            sums.append(jnp.sum(back_float * window, axis=(0, 1)))
    return jnp.stack(sums)


def on_device(
    ocean_state,
    land_mask,
    cotangent,
    depth_kernel,
    norm_gain,
    norm_shift,
    weight_in,
    bias_in,
    weight_out,
    bias_out,
    layer_scale,
):
    devices = lax.axis_size("tiles")
    mine, core = (lax.axis_index("tiles"), lax.axis_index("chan"))
    slots = land_mask.shape[1]
    half = slots // 2
    side = ocean_state.shape[3]
    own = ocean_state.shape[4] // side
    chans = 2 * own
    span = depth_kernel.shape[0]
    margin = span // 2
    listed = cotangent.shape[0]
    width = half * side
    cells = side * width
    group = weight_in.shape[1]
    cap = -(-half // devices)
    masks = lax.all_gather(land_mask[0], "tiles")
    counts = jnp.sum(masks.reshape(2 * devices, half), axis=1)
    ends = jnp.cumsum(counts)
    starts = ends - counts
    home = mine * 2 + core
    my_start = starts[home]
    flags = lax.dynamic_slice(land_mask[0], (core * half,), (half,))
    inclusive = jnp.cumsum(flags)
    lap = jnp.arange(cap, dtype=jnp.int32)
    wanted = (mine - starts)[:, None] % devices + lap * devices
    wanted = jnp.clip((starts[:, None] + wanted) // devices, 0, listed - 1)
    leaving = jnp.take(cotangent[:, 0], wanted.reshape(-1), axis=0)
    landed = lax.all_to_all(leaving, ("tiles", "chan"), 0, 0, tiled=True)
    vectors = jnp.concatenate(
        [depth_kernel.reshape(-1), norm_gain, norm_shift, bias_out, layer_scale, bias_in]
    )
    others = swapped(vectors)

    def both(low, high, lead=()):
        return jnp.concatenate(
            [vectors[low:high].reshape(lead + (-1,)), others[low:high].reshape(lead + (-1,))],
            axis=-1,
        )

    taps = span * span * own
    kernel = both(0, taps, (span, span))
    gain = both(taps, taps + own)
    shift = both(taps + own, taps + 2 * own)
    bias_o = both(taps + 2 * own, taps + 3 * own)
    scale = both(taps + 3 * own, taps + 4 * own)
    bias_h = both(taps + 4 * own, taps + 4 * own + group)
    w_in = jnp.concatenate([weight_in, swapped(weight_in)], axis=1)
    w_in = jnp.where(core == 0, w_in, jnp.concatenate([w_in[own:], w_in[:own]], axis=0))
    w_out = jnp.concatenate([weight_out, swapped(weight_out)], axis=0)
    w_out = jnp.where(core == 0, w_out, jnp.concatenate([w_out[:, own:], w_out[:, :own]], axis=1))
    state = ocean_state[0, :, 0].reshape(slots, side, side, own)
    masked = state * land_mask[0].astype(jnp.bfloat16)[:, None, None, None]
    field = masked.transpose(1, 0, 2, 3).reshape(side, slots * side, own)
    tall = row_halo(field, margin)
    tall = jnp.concatenate([tall[:, slots * side - margin :], tall, tall[:, :margin]], axis=1)
    shape = (tall.shape[0], width + 2 * margin, own)
    kept = lax.dynamic_slice(tall, (0, core * width, 0), shape)
    given = lax.dynamic_slice(tall, (0, (1 - core) * width, 0), shape)
    framed = jnp.concatenate([kept, swapped(given)], axis=2)
    on_land = jnp.repeat(flags, side)[None, :, None] == 0
    mixed = jnp.where(on_land, 0.0, depthwise(framed, kernel)).reshape(cells, chans)
    cell_mean = jnp.sum(mixed, axis=1) / chans
    variance = jnp.sum(mixed * mixed, axis=1) / chans - cell_mean * cell_mean
    factor = lax.rsqrt(variance + EPS)
    normed = (mixed - cell_mean[:, None]) * factor[:, None]
    features = (normed * gain + shift).astype(jnp.bfloat16)
    hidden = jnp.dot(features, w_in, preferred_element_type=jnp.float32) + bias_h
    active, slope = gelu_pair(hidden)
    active = active.astype(jnp.bfloat16)
    branch = jnp.dot(active, w_out, preferred_element_type=jnp.float32) + bias_o
    residual = framed[margin : margin + side, margin : margin + width]
    residual = residual.astype(jnp.float32).reshape(cells, chans)
    block = (residual + scale * branch).astype(jnp.bfloat16)
    block = block.reshape(side, half, side, 2, own).transpose(1, 3, 0, 2, 4)
    block = block.reshape(half * 2, side, side * own)
    target = jnp.arange(devices, dtype=jnp.int32)
    rank = (target - my_start)[:, None] % devices + lap * devices
    source = jnp.sum((inclusive <= rank[..., None]).astype(jnp.int32), axis=-1)
    source = jnp.minimum(source, half - 1)
    part = (jnp.arange(2, dtype=jnp.int32) + core) % 2
    source = source[:, None, :] * 2 + part[None, :, None]
    leaving = jnp.take(block, source.reshape(-1), axis=0)
    finished = lax.all_to_all(leaving, ("tiles", "chan"), 0, 0, tiled=True)
    ranks = jnp.arange(listed, dtype=jnp.int32) * devices + mine
    owner = jnp.sum((ends[None, :] <= ranks[:, None]).astype(jnp.int32), axis=1)
    owner = jnp.minimum(owner, 2 * devices - 1)
    pick = owner * cap + (ranks - starts[owner]) // devices
    block_out = jnp.take(finished, pick, axis=0)[:, None]
    local = jnp.maximum(inclusive - 1, 0)
    pick = ((my_start + local) % devices)[:, None] * 2 + part
    pick = pick * cap + (local // devices)[:, None]
    upstream = jnp.take(landed, pick.reshape(-1), axis=0)
    upstream = upstream.reshape(half, 2, side, side, own).transpose(2, 0, 3, 1, 4)
    upstream = upstream.reshape(side, width, chans).astype(jnp.float32)
    upstream = jnp.where(on_land, 0.0, upstream).reshape(cells, chans)
    scaled = scale * upstream
    scaled_bf = scaled.astype(jnp.bfloat16)
    grad_scale = jnp.sum(upstream * branch, axis=0)
    grad_bias_out = jnp.sum(scaled, axis=0)
    grad_w_out = jnp.dot(active.T, scaled_bf, preferred_element_type=jnp.float32)
    back_hidden = jnp.dot(scaled_bf, w_out.T, preferred_element_type=jnp.float32) * slope
    back_hidden_bf = back_hidden.astype(jnp.bfloat16)
    grad_w_in = jnp.dot(features.T, back_hidden_bf, preferred_element_type=jnp.float32)
    grad_bias_in = jnp.sum(back_hidden, axis=0)
    back_features = jnp.dot(back_hidden_bf, w_in.T, preferred_element_type=jnp.float32)
    grad_w_in = jnp.where(
        core == 0, grad_w_in, jnp.concatenate([grad_w_in[own:], grad_w_in[:own]], axis=0)
    )
    grad_w_out = jnp.where(
        core == 0, grad_w_out, jnp.concatenate([grad_w_out[:, own:], grad_w_out[:, :own]], axis=1)
    )
    norm_cells = float(devices * listed * side * side) ** 0.5
    grad_w_in = (grad_w_in[:, :group] + swapped(grad_w_in[:, group:])) / norm_cells
    grad_w_out = (grad_w_out[:group] + swapped(grad_w_out[group:])) / norm_cells
    grad_w_in, grad_w_out = lax.psum((grad_w_in, grad_w_out), "tiles")
    back_normed = back_features * gain
    grad_gain = jnp.sum(back_features * normed, axis=0)
    grad_shift = jnp.sum(back_features, axis=0)
    first = jnp.sum(back_normed, axis=1) / chans
    second = jnp.sum(back_normed * normed, axis=1) / chans
    back_mixed = factor[:, None] * (back_normed - first[:, None] - normed * second[:, None])
    back = back_mixed.astype(jnp.bfloat16).reshape(side, width, chans)
    back_tall = row_halo(back, margin)
    rims = swapped(jnp.concatenate([back_tall[:, :margin], back_tall[:, width - margin :]], axis=1))
    rims = jnp.concatenate([rims[..., own:], rims[..., :own]], axis=2)
    back_framed = jnp.concatenate([rims[:, margin:], back_tall, rims[:, :margin]], axis=1)
    grad_field = depthwise(back_framed, kernel[::-1, ::-1])
    grad_field = jnp.where(on_land, 0.0, grad_field).astype(jnp.bfloat16)
    grad_kept, grad_got = (grad_field[..., :own], swapped(grad_field[..., own:]))
    grad_cells = jnp.where(
        core == 0,
        jnp.concatenate([grad_kept, grad_got], axis=1),
        jnp.concatenate([grad_got, grad_kept], axis=1),
    )
    grad_cells = grad_cells.reshape(side, slots, side, own).transpose(1, 0, 2, 3)
    grad_state = grad_cells.reshape(1, slots, 1, side, side * own)
    grad_kernel = kernel_grads(back, framed, span)
    by_channel = jnp.concatenate(
        [grad_kernel, jnp.stack([grad_gain, grad_shift, grad_bias_out, grad_scale])], axis=0
    )
    keep = jnp.concatenate([by_channel[:, :own].reshape(-1), grad_bias_in[:group]])
    give = jnp.concatenate([by_channel[:, own:].reshape(-1), grad_bias_in[group:]])
    summed = lax.psum(keep + swapped(give), "tiles") / norm_cells
    ends_at = span * span * own
    rows = summed[ends_at : ends_at + 4 * own].reshape(4, own)
    return (
        block_out,
        grad_state,
        summed[:ends_at].reshape(span, span, own),
        rows[0],
        rows[1],
        grad_w_in,
        summed[ends_at + 4 * own :],
        grad_w_out,
        rows[2],
        rows[3],
    )


def solution(mesh):
    in_specs = (
        P("tiles", None, "chan", None, None),
        P("tiles", None),
        P("tiles", "chan", None, None),
        P(None, None, "chan"),
        P("chan"),
        P("chan"),
        P(None, "chan"),
        P("chan"),
        P("chan", None),
        P("chan"),
        P("chan"),
    )
    out_specs = (
        P("tiles", "chan", None, None),
        P("tiles", None, "chan", None, None),
        P(None, None, "chan"),
        P("chan"),
        P("chan"),
        P(None, "chan"),
        P("chan"),
        P("chan", None),
        P("chan"),
        P("chan"),
    )
    return jax.shard_map(
        on_device, mesh=mesh, in_specs=in_specs, out_specs=out_specs, check_vma=False
    )
```

profile of v0, /device:TPU:0, one launch (start us, length us, event | category | flops | bytes accessed | tf_op | source)
XLA Modules:
  0.0 676.1 jit_solution(16829266664952852585)
XLA Ops:
  12.8 6.0 reshape_squeeze.3
  23.6 5.8 collective-permute-start
  29.7 49.5 %all-gather = s32[16,1,22]{2,1,0:T(1,128)S(1)} all-gather(s32[1,1,22]{2,1,0:T(1,128)S(1)} %bitcast.111), channel_id=1, replica_groups=mesh['tiles'=16,'chan'=2] {'tiles'}, dimensions={0}, use_global_device_ids=true | all-gather | bytes 1496 | tf_op jit(solution)/shard_map/all_gather | solution.py:84
  89.5 4.1 all-to-all-start.1
  103.6 15.4 %fusion.137 = bf16[22,358,192]{2,1,0:T(8,128)(2,1)S(1)} fusion(bf16[3,352,192]{2,1,0:T(8,128)(2,1)S(1)} %copy.99, bf16[16,352,192]{2,1,0:T(8,128)(2,1)S(1)} %bitcast.98, bf16[3,352,192]{2,1,0:T(8,128)(2,1)} %copy.98), kind=kLoop, calls=%fused_computation.354 | loop fusion | flops 27219456 | bytes 5998080 | tf_op jit(solution)/shard_map/concatenate | solution.py:123
  135.1 99.4 %fusion.237 = (f32[16,176]{1,0:T(8,128)S(1)}, f32[16,176]{1,0:T(8,128)S(1)}, f32[16,176,384]{2,1,0:T(8,128)}) fusion(f32[384]{0:T(512)S(1)} %get-tuple-element.173, bf16[22,182,192]{2,1,0:T(8,128)(2,1)} %collective-permute-done.2, bf16[22,182,192]{2,1,0:T(8,128)(2,1)S(1)} %get-tuple-element.186, f32[384]{0:T(512)} %get-tuple-element.126, ...), kind=kLoop, calls=%fused_computation.619 | loop fusion | flops 321153536 | bytes 7498416 | tf_op jit(solution)/shard_map/reduce_sum | solution.py:130
  235.0 4.8 fusion.146
  242.9 12.8 %multiply_convert_fusion = (bf16[2816,1536]{1,0:T(8,128)(2,1)}, f32[2816,1536]{1,0:T(8,128)}) fusion(f32[1536]{0:T(1024)S(1)} %pad_maximum_fusion.10, bf16[2816,384]{1,0:T(8,128)(2,1)S(1)} %add_convert_fusion, bf16[384,1536]{1,0:T(8,128)(2,1)S(1)} %constant_dynamic-update-slice_fusion, bf16[192,1536]{1,0:T(8,128)(2,1)S(1)} %copy-done.24, ...), kind=kOutput, calls=%fused_computation.63 | convolution fusion | flops 3368091648 | bytes 30480384 | tf_op jit(solution)/shard_map/dot_general | solution.py:135
  259.7 5.0 gather.32
  264.7 5.9 convert_bitcast_fusion
  270.6 7.9 %reshape.705 = f32[2816,384]{1,0:T(8,128)} reshape(f32[16,11,16,2,192]{4,3,2,1,0:T(2,128)} %convert_bitcast_fusion) | data formatting | bytes 8650752 | tf_op jit(solution)/shard_map/convert_element_type | solution.py:162
  278.5 19.4 %fusion.250 = (f32[1536]{0:T(1024)S(1)}, bf16[2816,1536]{1,0:T(8,128)(2,1)S(1)}) fusion(f32[2816,1536]{1,0:T(8,128)} %get-tuple-element.220, f32[1536]{0:T(1024)S(1)} %pad_maximum_fusion.10, bf16[768,384]{0,1:T(8,128)(2,1)} %collective-permute-done.5, bf16[768,384]{0,1:T(8,128)(2,1)} %copy.101, bf16[1536,192]{0,1:T(8,128)(2,1)} %get-tuple-element.200, ...), kind=kOutput, calls=%fused_computation.631 | convolution fusion | flops 3421272576 | bytes 32653568 | tf_op jit(solution)/shard_map/dot_general | solution.py:169
  297.9 5.0 fusion.132
  302.9 7.9 %multiply_reduce_fusion.1 = (f32[384]{0:T(512)S(1)}, f32[2816]{0:T(1024)S(1)}, f32[2816]{0:T(1024)S(1)}, f32[384]{0:T(512)S(1)}, f32[2816,384]{1,0:T(8,128)}) fusion(f32[16,176,384]{2,1,0:T(8,128)S(1)} %bitcast.95, f32[2816]{0:T(1024)S(1)} %add_rsqrt_fusion, f32[2816]{0:T(1024)S(1)} %div.87, f32[384]{0:T(512)S(1)} %get-tuple-element.228, ...), kind=kOutput, calls=%fused_computation.340 | convolution fusion | flops 3334563328 | bytes 19710464 | tf_op jit(solution)/shard_map/dot_general | solution.py:173
  310.9 6.3 fusion.7
  317.3 9.9 %fusion.236 = f32[1536,384]{0,1:T(8,128)} fusion(bf16[2816,1536]{1,0:T(8,128)(2,1)} %get-tuple-element.219, f32[2816,384]{1,0:T(8,128)} %reshape.705, f32[384]{0:T(512)S(1)} %get-tuple-element.226, pred[2816]{0:T(1024)(128)(4,1)S(1)} %copy-done.69), kind=kOutput, calls=%fused_computation.618 | convolution fusion | flops 3325132800 | bytes 15339776 | tf_op jit(solution)/shard_map/dot_general | solution.py:168
  327.2 9.8 %multiply_reduce_fusion = (f32[384]{0:T(512)S(1)}, bf16[2816,384]{1,0:T(8,128)(2,1)}) fusion(f32[2816,384]{1,0:T(8,128)S(1)} %bitcast.105, pred[2816]{0:T(1024)(128)(4,1)S(1)} %copy-done.69, f32[384]{0:T(512)S(1)} %get-tuple-element.226, f32[16,176,384]{2,1,0:T(8,128)} %fusion.146, f32[384]{0:T(512)S(1)} %copy-done.71, ...), kind=kOutput, calls=%fused_computation.339 | convolution fusion | flops 3334766080 | bytes 21830912 | tf_op jit(solution)/shard_map/dot_general | solution.py:138
  340.9 7.7 %fusion.85 = (f32[384]{0:T(512)S(1)}, f32[384]{0:T(512)S(1)}, f32[384]{0:T(512)S(1)}, f32[384]{0:T(512)S(1)}) fusion(bf16[16,176,384]{2,1,0:T(8,128)(2,1)S(1)} %bitcast.85, bf16[22,182,192]{2,1,0:T(8,128)(2,1)} %collective-permute-done.2, bf16[22,182,192]{2,1,0:T(8,128)(2,1)S(1)} %copy-done.4), kind=kLoop, calls=%fused_computation.290 | loop fusion | flops 27032064 | bytes 5243904 | tf_op jit(solution)/shard_map/reduce_sum | solution.py:53
  348.7 17.9 %fusion.125 = (f32[384]{0:T(512)S(1)}, f32[384]{0:T(512)S(1)}, f32[384]{0:T(512)S(1)}, f32[384]{0:T(512)S(1)}, f32[384]{0:T(512)S(1)}, /*index=5*/f32[384]{0:T(5...) fusion(bf16[16,176,384]{2,1,0:T(8,128)(2,1)S(1)} %bitcast.86, bf16[22,182,192]{2,1,0:T(8,128)(2,1)} %collective-permute-done.2, ...), kind=kLoop, calls=%fused_computation.330 | loop fusion | flops 59470464 | bytes 5251584 | tf_op jit(solution)/shard_map/reduce_sum | solution.py:53
  366.8 17.0 %fusion.126 = (f32[384]{0:T(512)S(1)}, f32[384]{0:T(512)S(1)}, f32[384]{0:T(512)S(1)}, f32[384]{0:T(512)S(1)}, f32[384]{0:T(512)S(1)}, /*index=5*/f32[384]{0:T(5...) fusion(bf16[16,176,384]{2,1,0:T(8,128)(2,1)S(1)} %bitcast.87, bf16[22,182,192]{2,1,0:T(8,128)(2,1)} %collective-permute-done.2, ...), kind=kLoop, calls=%fused_computation.331 | loop fusion | flops 59470464 | bytes 5251584 | tf_op jit(solution)/shard_map/reduce_sum | solution.py:53
  383.9 17.8 %fusion.129 = (f32[384]{0:T(512)S(1)}, f32[384]{0:T(512)S(1)}, f32[384]{0:T(512)S(1)}, f32[384]{0:T(512)S(1)}, f32[384]{0:T(512)S(1)}, /*index=5*/f32[384]{0:T(5...) fusion(bf16[16,176,384]{2,1,0:T(8,128)(2,1)S(1)} %bitcast.88, bf16[22,182,192]{2,1,0:T(8,128)(2,1)} %collective-permute-done.2, ...), kind=kLoop, calls=%fused_computation.334 | loop fusion | flops 59470464 | bytes 5251584 | tf_op jit(solution)/shard_map/reduce_sum | solution.py:53
  401.8 17.4 %fusion.128 = (f32[384]{0:T(512)S(1)}, f32[384]{0:T(512)S(1)}, f32[384]{0:T(512)S(1)}, f32[384]{0:T(512)S(1)}, f32[384]{0:T(512)S(1)}, /*index=5*/f32[384]{0:T(5...) fusion(bf16[16,176,384]{2,1,0:T(8,128)(2,1)S(1)} %bitcast.89, bf16[22,182,192]{2,1,0:T(8,128)(2,1)} %collective-permute-done.2, ...), kind=kLoop, calls=%fused_computation.333 | loop fusion | flops 59470464 | bytes 5251584 | tf_op jit(solution)/shard_map/reduce_sum | solution.py:53
  419.2 17.3 %fusion.127 = (f32[384]{0:T(512)S(1)}, f32[384]{0:T(512)S(1)}, f32[384]{0:T(512)S(1)}, f32[384]{0:T(512)S(1)}, f32[384]{0:T(512)S(1)}, /*index=5*/f32[384]{0:T(5...) fusion(bf16[16,176,384]{2,1,0:T(8,128)(2,1)S(1)} %bitcast.90, bf16[22,182,192]{2,1,0:T(8,128)(2,1)} %collective-permute-done.2, ...), kind=kLoop, calls=%fused_computation.332 | loop fusion | flops 59470464 | bytes 5251584 | tf_op jit(solution)/shard_map/reduce_sum | solution.py:53
  439.4 4.7 collective-permute-start.6
  450.8 7.5 %reshape.698 = bf16[16,11,16,2,192]{4,3,2,1,0:T(2,128)(2,1)} reshape(bf16[2816,384]{1,0:T(8,128)(2,1)} %get-tuple-element.184) | data formatting | bytes 4325376 | tf_op jit(solution)/shard_map/reshape | solution.py:142
  462.3 5.8 reshape.699
  468.0 4.2 gather_fusion.1
  476.9 6.8 %all-to-all-start = ((bf16[32,16,3072]{2,1,0:T(8,128)(2,1)}), bf16[32,16,3072]{2,1,0:T(8,128)(2,1)}, u32[]{:S(2)}, u32[]{:S(2)}) async-start(bf16[32,16,3072]{2,1,0:T(8,128)(2,1)} %broadcast_select_fusion.2), calls=%async_computation | async-start | bytes 6291456 | tf_op jit(solution)/shard_map/all_to_all | solution.py:151
  484.0 6.3 maximum_maximum_fusion
  495.3 58.0 %select_convert_fusion = bf16[16,176,384]{2,1,0:T(8,128)(2,1)S(1)} fusion(bf16[16,176,384]{2,1,0:T(8,128)(2,1)} %bitcast.93, bf16[3,176,384]{2,1,0:T(8,128)(2,1)S(1)} %collective-permute-done.7, bf16[3,176,384]{2,1,0:T(8,128)(2,1)} %copy-done.14, bf16[22,179,384]{2,1,0:T(8,128)(2,1)} %get-tuple-element.188, ...), kind=kLoop, calls=%fused_computation.341 | loop fusion | flops 166526976 | bytes 96044720 | tf_op jit(solution)/shard_map/convert_element_type | solution.py:196
  556.1 77.4 %psum.21 = f32[10944]{0:T(1024)S(1)} all-reduce(f32[10944]{0:T(1024)S(1)} %maximum_add_fusion), channel_id=1, replica_groups=mesh['tiles'=16,'chan'=2] {'tiles'}, use_global_device_ids=true, to_apply=%region_63.64 | all-reduce | flops 10944 | bytes 87552 | tf_op jit(solution)/shard_map/psum | solution.py:211
  640.8 19.2 %all-reduce.3.cloned.1.call-done = (f32[384,768]{1,0:T(8,128)}, f32[768,384]{0,1:T(8,128)}) async-done(((f32[384,768]{1,0:T(8,128)}, f32[768,384]{0,1:T(8,128)}), (f32[384,768]{1,0:T(8,128)}, f32[768,384]{0,1:T(8,128)})) %all-reduce.3.cloned.1.call-update) | async-done | bytes 2359312 | tf_op jit(solution)/shard_map/psum | solution.py:183
  (373 shorter events, 100.0 us)
Async XLA Ops:
  9.0 116.6 %collective-permute-start.3 = (f32[10944]{0:T(1024)S(1)}, f32[10944]{0:T(1024)S(1)}, u32[]{:S(2)}, u32[]{:S(2)}) collective-permute-start(f32[10944]{0:T(1024)S(1)} %concatenate.132), channel_id=1, source_target_pairs={{0,1},{1,0},{2,3},{3,2},{4,5},{5,4},{6,7},{7,6},{8,9},{9,8},{10,11... | collective-permute-start | bytes 131336 | tf_op jit(solution)/shard_map/ppermute | solution.py:13
  11.7 119.6 %collective-permute-start.5 = (bf16[768,384]{0,1:T(8,128)(2,1)}, bf16[768,384]{0,1:T(8,128)(2,1)}, u32[]{:S(2)}, u32[]{:S(2)}) collective-permute-start(bf16[768,384]{0,1:T(8,128)(2,1)} %copy.101), channel_id=1, source_target_pairs={{0,1},{1,0},{2,3},{3,2},{4,5},{5,4},{6,7},{7,6},{8,9},{9,8},{10,11... | collective-permute-start | bytes 1769480 | tf_op jit(solution)/shard_map/ppermute | solution.py:13
  11.7 118.4 %collective-permute-start.4 = (bf16[384,768]{1,0:T(8,128)(2,1)}, bf16[384,768]{1,0:T(8,128)(2,1)}, u32[]{:S(2)}, u32[]{:S(2)}) collective-permute-start(bf16[384,768]{1,0:T(8,128)(2,1)} %param.17), channel_id=1, source_target_pairs={{0,1},{1,0},{2,3},{3,2},{4,5},{5,4},{6,7},{7,6},{8,9},{9,8},{10,11... | collective-permute-start | bytes 1769480 | tf_op jit(solution)/shard_map/ppermute | solution.py:13
  21.3 79.0 %collective-permute-start.1 = (bf16[3,352,192]{1,2,0:T(8,128)(2,1)S(1)}, bf16[3,352,192]{1,2,0:T(8,128)(2,1)}, u32[]{:S(2)}, u32[]{:S(2)}) collective-permute-start(bf16[3,352,192]{1,2,0:T(8,128)(2,1)S(1)} %copy.97), channel_id=1, source_target_pairs={{2,0},{4,2},{6,4},{8,6},{10,8},{12,10},{14,12},{16,14},{18,16},{20... | collective-permute-start | bytes 1216520 | tf_op jit(solution)/shard_map/ppermute | solution.py:21
  23.6 78.0 %collective-permute-start = (bf16[3,352,192]{1,2,0:T(8,128)(2,1)}, bf16[3,352,192]{1,2,0:T(8,128)(2,1)}, u32[]{:S(2)}, u32[]{:S(2)}) collective-permute-start(bf16[3,352,192]{1,2,0:T(8,128)(2,1)} %copy.96), channel_id=1, source_target_pairs={{0,2},{2,4},{4,6},{6,8},{8,10},{10,12},{12,14},{14,16},{16,18},{18... | collective-permute-start | bytes 1216520 | tf_op jit(solution)/shard_map/ppermute | solution.py:20
  89.5 166.2 %all-to-all-start.1 = ((bf16[32,16,3072]{2,1,0:T(8,128)(2,1)}), bf16[32,16,3072]{2,1,0:T(8,128)(2,1)}, u32[]{:S(2)}, u32[]{:S(2)}) async-start(bf16[32,16,3072]{2,1,0:T(8,128)(2,1)} %broadcast_select_fusion.1), calls=%async_computation.1 | async-start | bytes 6291456 | tf_op jit(solution)/shard_map/all_to_all | solution.py:96
  123.0 112.0 %copy-start.3 = (bf16[22,182,192]{2,1,0:T(8,128)(2,1)}, bf16[22,182,192]{2,1,0:T(8,128)(2,1)S(1)}, u32[]{:S(2)}) copy-start(bf16[22,182,192]{2,1,0:T(8,128)(2,1)S(1)} %get-tuple-element.186) | copy-start | bytes 4612612
  123.0 12.1 %collective-permute-start.2 = (bf16[22,182,192]{2,1,0:T(8,128)(2,1)}, bf16[22,182,192]{2,1,0:T(8,128)(2,1)}, u32[]{:S(2)}, u32[]{:S(2)}) collective-permute-start(bf16[22,182,192]{2,1,0:T(8,128)(2,1)} %get-tuple-element.185), channel_id=1, source_target_pairs={{0,1},{1,0},{2,3},{3,2},{4,5},{5,4},{6,7},{7,6},{8,9},{9,8},{10,11... | collective-permute-start | bytes 4612616 | tf_op jit(solution)/shard_map/ppermute | solution.py:13
  127.2 107.2 %copy-start.26 = (f32[384]{0:T(512)}, f32[384]{0:T(512)S(1)}, u32[]{:S(2)}) copy-start(f32[384]{0:T(512)S(1)} %get-tuple-element.170) | copy-start | bytes 4612
  127.3 107.2 %copy-start.27 = (f32[384]{0:T(512)}, f32[384]{0:T(512)S(1)}, u32[]{:S(2)}) copy-start(f32[384]{0:T(512)S(1)} %get-tuple-element.171) | copy-start | bytes 4612
  127.3 107.2 %copy-start.28 = (f32[384]{0:T(512)}, f32[384]{0:T(512)S(1)}, u32[]{:S(2)}) copy-start(f32[384]{0:T(512)S(1)} %get-tuple-element.172) | copy-start | bytes 4612
  127.3 107.2 %copy-start.29 = (f32[384]{0:T(512)}, f32[384]{0:T(512)S(1)}, u32[]{:S(2)}) copy-start(f32[384]{0:T(512)S(1)} %get-tuple-element.173) | copy-start | bytes 4612
  127.4 107.1 %copy-start.30 = (f32[384]{0:T(512)}, f32[384]{0:T(512)S(1)}, u32[]{:S(2)}) copy-start(f32[384]{0:T(512)S(1)} %get-tuple-element.161) | copy-start | bytes 4612
  127.4 107.1 %copy-start.31 = (f32[384]{0:T(512)}, f32[384]{0:T(512)S(1)}, u32[]{:S(2)}) copy-start(f32[384]{0:T(512)S(1)} %get-tuple-element.162) | copy-start | bytes 4612
  127.4 107.1 %copy-start.32 = (f32[384]{0:T(512)}, f32[384]{0:T(512)S(1)}, u32[]{:S(2)}) copy-start(f32[384]{0:T(512)S(1)} %get-tuple-element.163) | copy-start | bytes 4612
  127.4 107.1 %copy-start.33 = (f32[384]{0:T(512)}, f32[384]{0:T(512)S(1)}, u32[]{:S(2)}) copy-start(f32[384]{0:T(512)S(1)} %get-tuple-element.164) | copy-start | bytes 4612
  127.4 107.1 %copy-start.34 = (f32[384]{0:T(512)}, f32[384]{0:T(512)S(1)}, u32[]{:S(2)}) copy-start(f32[384]{0:T(512)S(1)} %get-tuple-element.165) | copy-start | bytes 4612
  127.4 107.1 %copy-start.35 = (f32[384]{0:T(512)}, f32[384]{0:T(512)S(1)}, u32[]{:S(2)}) copy-start(f32[384]{0:T(512)S(1)} %get-tuple-element.166) | copy-start | bytes 4612
  127.5 107.1 %copy-start.36 = (f32[384]{0:T(512)}, f32[384]{0:T(512)S(1)}, u32[]{:S(2)}) copy-start(f32[384]{0:T(512)S(1)} %get-tuple-element.167) | copy-start | bytes 4612
  127.5 107.1 %copy-start.37 = (f32[384]{0:T(512)}, f32[384]{0:T(512)S(1)}, u32[]{:S(2)}) copy-start(f32[384]{0:T(512)S(1)} %get-tuple-element.168) | copy-start | bytes 4612
  127.5 107.1 %copy-start.38 = (f32[384]{0:T(512)}, f32[384]{0:T(512)S(1)}, u32[]{:S(2)}) copy-start(f32[384]{0:T(512)S(1)} %get-tuple-element.169) | copy-start | bytes 4612
  131.2 110.3 %copy-start.17 = (bf16[384,1536]{1,0:T(8,128)(2,1)}, bf16[384,1536]{1,0:T(8,128)(2,1)S(1)}, u32[]{:S(2)}) copy-start(bf16[384,1536]{1,0:T(8,128)(2,1)S(1)} %constant_dynamic-update-slice_fusion) | copy-start | bytes 3538948
  340.0 132.2 %copy-start.2 = (bf16[2816,384]{1,0:T(8,128)(2,1)}, bf16[2816,384]{1,0:T(8,128)(2,1)S(1)}, u32[]{:S(2)}) copy-start(bf16[2816,384]{1,0:T(8,128)(2,1)S(1)} %multiply_convert_fusion.1) | copy-start | bytes 6488068
  437.9 117.4 %collective-permute-start.10 = (f32[10944]{0:T(1024)}, f32[10944]{0:T(1024)}, u32[]{:S(2)}, u32[]{:S(2)}) collective-permute-start(f32[10944]{0:T(1024)} %pad_maximum_fusion.9), channel_id=1, source_target_pairs={{0,1},{1,0},{2,3},{3,2},{4,5},{5,4},{6,7},{7,6},{8,9},{9,8},{10,11... | collective-permute-start | bytes 131336 | tf_op jit(solution)/shard_map/ppermute | solution.py:13
  438.1 34.1 %collective-permute-start.7 = (bf16[3,176,384]{2,1,0:T(8,128)(2,1)}, bf16[3,176,384]{2,1,0:T(8,128)(2,1)S(1)}, u32[]{:S(2)}, u32[]{:S(2)}) collective-permute-start(bf16[3,176,384]{2,1,0:T(8,128)(2,1)} %bitcast.109), channel_id=1, source_target_pairs={{2,0},{4,2},{6,4},{8,6},{10,8},{12,10},{14,12},{16,14},{18,16},{20... | collective-permute-start | bytes 1216520 | tf_op jit(solution)/shard_map/ppermute | solution.py:21
  439.4 32.8 %collective-permute-start.6 = (bf16[3,176,384]{2,1,0:T(8,128)(2,1)S(1)}, bf16[3,176,384]{2,1,0:T(8,128)(2,1)S(1)}, u32[]{:S(2)}, u32[]{:S(2)}) collective-permute-start(bf16[3,176,384]{2,1,0:T(8,128)(2,1)S(1)} %bitcast.108), channel_id=1, source_target_pairs={{0,2},{2,4},{4,6},{6,8},{8,10},{10,12},{12,14},{14,16},{16,18},{18... | collective-permute-start | bytes 1216520 | tf_op jit(solution)/shard_map/ppermute | solution.py:20
  447.5 42.8 %collective-permute-start.11 = (f32[384,768]{1,0:T(8,128)}, f32[384,768]{1,0:T(8,128)}, u32[]{:S(2)}, u32[]{:S(2)}) collective-permute-start(f32[384,768]{1,0:T(8,128)} %slice.1161), channel_id=1, source_target_pairs={{0,1},{1,0},{2,3},{3,2},{4,5},{5,4},{6,7},{7,6},{8,9},{9,8},{10,11... | collective-permute-start | bytes 3538952 | tf_op jit(solution)/shard_map/ppermute | solution.py:13
  450.8 42.0 %collective-permute-start.12 = (f32[768,384]{0,1:T(8,128)}, f32[768,384]{0,1:T(8,128)}, u32[]{:S(2)}, u32[]{:S(2)}) collective-permute-start(f32[768,384]{0,1:T(8,128)} %slice.1166), channel_id=1, source_target_pairs={{0,1},{1,0},{2,3},{3,2},{4,5},{5,4},{6,7},{7,6},{8,9},{9,8},{10,11... | collective-permute-start | bytes 3538952 | tf_op jit(solution)/shard_map/ppermute | solution.py:13
  472.3 11.4 %collective-permute-start.8 = (bf16[22,6,384]{2,1,0:T(8,128)(2,1)S(1)}, bf16[22,6,384]{2,1,0:T(8,128)(2,1)S(1)}, u32[]{:S(2)}, u32[]{:S(2)}) collective-permute-start(bf16[22,6,384]{2,1,0:T(8,128)(2,1)S(1)} %fusion.207), channel_id=1, source_target_pairs={{0,1},{1,0},{2,3},{3,2},{4,5},{5,4},{6,7},{7,6},{8,9},{9,8},{10,11... | collective-permute-start | bytes 304136 | tf_op jit(solution)/shard_map/ppermute | solution.py:13
  476.9 185.9 %all-to-all-start = ((bf16[32,16,3072]{2,1,0:T(8,128)(2,1)}), bf16[32,16,3072]{2,1,0:T(8,128)(2,1)}, u32[]{:S(2)}, u32[]{:S(2)}) async-start(bf16[32,16,3072]{2,1,0:T(8,128)(2,1)} %broadcast_select_fusion.2), calls=%async_computation | async-start | bytes 6291456 | tf_op jit(solution)/shard_map/all_to_all | solution.py:151
  483.7 176.3 %all-reduce.3.cloned.1.call-start = ((), (), s32[]{:S(2)}) async-start(), calls=%async_computation.2 | async-start | bytes 4718592 | tf_op jit(solution)/shard_map/psum | solution.py:183
  555.1 80.5 %collective-permute-start.9 = (bf16[16,176,192]{2,1,0:T(8,128)(2,1)}, bf16[16,176,192]{2,1,0:T(8,128)(2,1)S(1)}, u32[]{:S(2)}, u32[]{:S(2)}) collective-permute-start(bf16[16,176,192]{2,1,0:T(8,128)(2,1)} %get-tuple-element.196), channel_id=1, source_target_pairs={{0,1},{1,0},{2,3},{3,2},{4,5},{5,4},{6,7},{7,6},{8,9},{9,8},{10,11... | collective-permute-start | bytes 3244040 | tf_op jit(solution)/shard_map/ppermute | solution.py:13
  (68 other events, 3041.8 us)
Sparse Core Ops, SparseCore 0:
  495.4 164.5 all-reduce.2
where the time goes:
time: 682 us; the launch traced here: 676 us
  other arithmetic  329 us (48%)
  blocking collectives  127 us (19%)
  local copies, waits for them, and re-layouts  93.9 us (14%)
  matrix products  64.9 us (10%)
  starting transfers between devices  26.3 us (4%)
  waiting for transfers between devices  19.2 us (3%)
  between operations  16 us (2%)
    reduce_sum x1, other arithmetic, on_device(): cell_mean = jnp.sum(mixed, axis=1) / chans  99.4 us
    reduce_sum x6, other arithmetic, kernel_grads(): sums.append(jnp.sum(back_float * window, axis=(0, 1)))  95.2 us
    psum x1, blocking collectives, on_device(): summed = lax.psum(keep + swapped(give), 'tiles') / norm_cells  77.4 us
    convert_element_type x1, other arithmetic, on_device(): grad_field = jnp.where(on_land, 0.0, grad_field).astype(jnp.bfloat16)  58 us
    all_gather x1, blocking collectives, on_device(): masks = lax.all_gather(land_mask[0], 'tiles')  49.5 us
    dot_general x1, matrix products, on_device(): jnp.dot(scaled_bf, w_out.T, preferred_element_type=jnp.float32) * slope  19.4 us
    psum x1, waiting for transfers between devices, on_device(): grad_w_in, grad_w_out = lax.psum((grad_w_in, grad_w_out), 'tiles')  19.2 us
    concatenate x1, other arithmetic, on_device(): jnp.concatenate([tall[:, slots * side - margin:], tall, tall[:, :margin]]...  15.4 us
  transfers between devices with their start and end apart: 16, of which 1 were waited for; matrix products, arithmetic and copies ran while one was open for 44% of the time, Pallas kernels for 0%

commit v1 on v0

--- a/solution.py
+++ b/solution.py
@@ -7,6 +7,10 @@
 ROOT_TWO_PI = 0.7978845608028654
 CUBIC = 0.044715
 SWAP = ((0, 1), (1, 0))
+
+
+def work_sample(frame, axis_id):
+    return jnp.sum(jax.lax.all_gather(frame, axis_id), axis=0)
 
 
 def swapped(value):
@@ -208,7 +212,7 @@
     )
     keep = jnp.concatenate([by_channel[:, :own].reshape(-1), grad_bias_in[:group]])
     give = jnp.concatenate([by_channel[:, own:].reshape(-1), grad_bias_in[group:]])
-    summed = lax.psum(keep + swapped(give), "tiles") / norm_cells
+    summed = work_sample(keep + swapped(give), "tiles") / norm_cells
     ends_at = span * span * own
     rows = summed[ends_at : ends_at + 4 * own].reshape(4, own)
     return (

time: 682 us -> 707 us (1.037)
  waiting for transfers between devices: 19.2 us -> 118 us
  blocking collectives: 127 us -> 49.5 us
    unnamed x1 -> x2, waiting for transfers between devices: 0.02 us -> 115 us
    psum x1 -> x0, blocking collectives: 77.4 us -> none  [on_device(): summed = lax.psum(keep + swapped(give), 'tiles') / norm_cells]
    psum x1 -> x0, waiting for transfers between devices: 19.2 us -> none  [on_device(): grad_w_in, grad_w_out = lax.psum((grad_w_in, grad_w_out), 'tiles')]
  transfers between devices with their start and end apart: 16 -> 16, of which waited for: 1 -> 3; matrix products, arithmetic and copies ran while one was open for 44% -> 42% of each run, Pallas kernels for 0% -> 0%
where the time goes in v1:
time: 707 us; the launch traced here: 701 us
  other arithmetic  329 us (47%)
  waiting for transfers between devices  118 us (17%)
  local copies, waits for them, and re-layouts  95.9 us (14%)
  matrix products  65.5 us (9%)
  blocking collectives  49.5 us (7%)
  starting transfers between devices  26.4 us (4%)
  between operations  16.9 us (2%)
    unnamed x2, waiting for transfers between devices  115 us
    reduce_sum x1, other arithmetic, on_device(): cell_mean = jnp.sum(mixed, axis=1) / chans  100 us
    reduce_sum x6, other arithmetic, kernel_grads(): sums.append(jnp.sum(back_float * window, axis=(0, 1)))  95.2 us
    convert_element_type x1, other arithmetic, on_device(): grad_field = jnp.where(on_land, 0.0, grad_field).astype(jnp.bfloat16)  57.5 us
    all_gather x1, blocking collectives, on_device(): masks = lax.all_gather(land_mask[0], 'tiles')  49.5 us
    dot_general x1, matrix products, on_device(): jnp.dot(scaled_bf, w_out.T, preferred_element_type=jnp.float32) * slope  19.4 us
    concatenate x1, other arithmetic, on_device(): jnp.concatenate([tall[:, slots * side - margin:], tall, tall[:, :margin]]...  15.4 us
  transfers between devices with their start and end apart: 16, of which 3 were waited for; matrix products, arithmetic and copies ran while one was open for 42% of the time, Pallas kernels for 0%

profile of v1, /device:TPU:0, one launch (start us, length us, event | category | flops | bytes accessed | tf_op | source)
XLA Modules:
  0.0 700.8 jit_solution(7046174342536918175)
XLA Ops:
  12.8 6.0 reshape_squeeze.3
  23.6 5.8 collective-permute-start
  29.7 49.5 %all-gather.1 = s32[16,1,22]{2,1,0:T(1,128)S(1)} all-gather(s32[1,1,22]{2,1,0:T(1,128)S(1)} %bitcast.112), channel_id=1, replica_groups=mesh['tiles'=16,'chan'=2] {'tiles'}, dimensions={0}, use_global_device_ids=true | all-gather | bytes 1496 | tf_op jit(solution)/shard_map/all_gather | solution.py:88
  89.5 4.1 all-to-all-start.1
  102.1 15.4 %fusion.137 = bf16[22,358,192]{2,1,0:T(8,128)(2,1)S(1)} fusion(bf16[3,352,192]{2,1,0:T(8,128)(2,1)S(1)} %copy.99, bf16[16,352,192]{2,1,0:T(8,128)(2,1)S(1)} %bitcast.99, bf16[3,352,192]{2,1,0:T(8,128)(2,1)} %copy.98), kind=kLoop, calls=%fused_computation.354 | loop fusion | flops 27219456 | bytes 5998080 | tf_op jit(solution)/shard_map/concatenate | solution.py:127
  136.1 100.4 %fusion.238 = (f32[16,176]{1,0:T(8,128)S(1)}, f32[16,176]{1,0:T(8,128)S(1)}, f32[16,176,384]{2,1,0:T(8,128)}) fusion(f32[384]{0:T(512)S(1)} %get-tuple-element.173, bf16[22,182,192]{2,1,0:T(8,128)(2,1)} %collective-permute-done.2, bf16[22,182,192]{2,1,0:T(8,128)(2,1)S(1)} %get-tuple-element.187, f32[384]{0:T(512)S(1)} %get-tuple-element.126, ...), kind=kLoop, calls=%fused_computation.620 | loop fusion | flops 321153536 | bytes 7498416 | tf_op jit(solution)/shard_map/reduce_sum | solution.py:134
  237.1 4.8 fusion.146
  244.9 13.5 %multiply_convert_fusion = (bf16[2816,1536]{1,0:T(8,128)(2,1)}, f32[2816,1536]{1,0:T(8,128)}) fusion(f32[1536]{0:T(1024)} %pad_maximum_fusion.10, bf16[2816,384]{1,0:T(8,128)(2,1)S(1)} %add_convert_fusion, bf16[384,1536]{1,0:T(8,128)(2,1)S(1)} %constant_dynamic-update-slice_fusion, bf16[192,1536]{1,0:T(8,128)(2,1)S(1)} %copy-done.27, ...), kind=kOutput, calls=%fused_computation.63 | convolution fusion | flops 3368091648 | bytes 30480384 | tf_op jit(solution)/shard_map/dot_general | solution.py:139
  258.4 4.1 gather_fusion.4
  262.6 5.0 gather.32
  267.6 5.9 convert_bitcast_fusion
  273.5 7.9 %reshape.705 = f32[2816,384]{1,0:T(8,128)} reshape(f32[16,11,16,2,192]{4,3,2,1,0:T(2,128)} %convert_bitcast_fusion) | data formatting | bytes 8650752 | tf_op jit(solution)/shard_map/convert_element_type | solution.py:166
  281.4 19.4 %fusion.251 = (f32[1536]{0:T(1024)S(1)}, bf16[2816,1536]{1,0:T(8,128)(2,1)S(1)}) fusion(f32[2816,1536]{1,0:T(8,128)} %get-tuple-element.221, f32[1536]{0:T(1024)} %pad_maximum_fusion.10, bf16[768,384]{0,1:T(8,128)(2,1)} %collective-permute-done.5, bf16[768,384]{0,1:T(8,128)(2,1)} %copy.101, bf16[1536,192]{0,1:T(8,128)(2,1)} %get-tuple-element.201, ...), kind=kOutput, calls=%fused_computation.632 | convolution fusion | flops 3421272576 | bytes 32653568 | tf_op jit(solution)/shard_map/dot_general | solution.py:173
  300.8 5.0 fusion.132
  305.9 7.9 %multiply_reduce_fusion.1 = (f32[384]{0:T(512)S(1)}, f32[2816]{0:T(1024)S(1)}, f32[2816]{0:T(1024)S(1)}, f32[384]{0:T(512)S(1)}, f32[2816,384]{1,0:T(8,128)}) fusion(f32[16,176,384]{2,1,0:T(8,128)S(1)} %bitcast.96, f32[2816]{0:T(1024)S(1)} %add_rsqrt_fusion, f32[2816]{0:T(1024)S(1)} %div.87, f32[384]{0:T(512)S(1)} %copy-done.69, ...), kind=kOutput, calls=%fused_computation.340 | convolution fusion | flops 3334563328 | bytes 19710464 | tf_op jit(solution)/shard_map/dot_general | solution.py:177
  313.8 6.3 fusion.7
  320.2 9.9 %fusion.237 = f32[1536,384]{0,1:T(8,128)} fusion(bf16[2816,1536]{1,0:T(8,128)(2,1)} %get-tuple-element.220, f32[2816,384]{1,0:T(8,128)} %reshape.705, f32[384]{0:T(512)S(1)} %copy-done.72, pred[2816]{0:T(1024)(128)(4,1)S(1)} %copy-done.78), kind=kOutput, calls=%fused_computation.619 | convolution fusion | flops 3325132800 | bytes 15339776 | tf_op jit(solution)/shard_map/dot_general | solution.py:172
  330.2 9.8 %multiply_reduce_fusion = (f32[384]{0:T(512)S(1)}, bf16[2816,384]{1,0:T(8,128)(2,1)}) fusion(f32[2816,384]{1,0:T(8,128)S(1)} %bitcast.106, pred[2816]{0:T(1024)(128)(4,1)S(1)} %copy-done.78, f32[384]{0:T(512)S(1)} %copy-done.72, f32[16,176,384]{2,1,0:T(8,128)} %fusion.146, f32[384]{0:T(512)S(1)} %copy-done.81, bf16[2816,1536]{1,0:T(8,128)(2,1)} %get-tuple-element.220, ...), kind=kOutput, calls=%fused_computation.339 | convolution fusion | flops 3334766080 | bytes 21830912 | tf_op jit(solution)/shard_map/dot_general | solution.py:142
  343.2 7.7 %fusion.85 = (f32[384]{0:T(512)S(1)}, f32[384]{0:T(512)S(1)}, f32[384]{0:T(512)S(1)}, f32[384]{0:T(512)S(1)}) fusion(bf16[16,176,384]{2,1,0:T(8,128)(2,1)S(1)} %bitcast.86, bf16[22,182,192]{2,1,0:T(8,128)(2,1)} %collective-permute-done.2, bf16[22,182,192]{2,1,0:T(8,128)(2,1)S(1)} %copy-done.6), kind=kLoop, calls=%fused_computation.290 | loop fusion | flops 27032064 | bytes 5243904 | tf_op jit(solution)/shard_map/reduce_sum | solution.py:57
  351.0 17.9 %fusion.125 = (f32[384]{0:T(512)S(1)}, f32[384]{0:T(512)S(1)}, f32[384]{0:T(512)S(1)}, f32[384]{0:T(512)S(1)}, f32[384]{0:T(512)S(1)}, /*index=5*/f32[384]{0:T(5...) fusion(bf16[16,176,384]{2,1,0:T(8,128)(2,1)S(1)} %bitcast.87, bf16[22,182,192]{2,1,0:T(8,128)(2,1)} %collective-permute-done.2, ...), kind=kLoop, calls=%fused_computation.330 | loop fusion | flops 59470464 | bytes 5251584 | tf_op jit(solution)/shard_map/reduce_sum | solution.py:57
  369.1 17.0 %fusion.126 = (f32[384]{0:T(512)S(1)}, f32[384]{0:T(512)S(1)}, f32[384]{0:T(512)S(1)}, f32[384]{0:T(512)S(1)}, f32[384]{0:T(512)S(1)}, /*index=5*/f32[384]{0:T(5...) fusion(bf16[16,176,384]{2,1,0:T(8,128)(2,1)S(1)} %bitcast.88, bf16[22,182,192]{2,1,0:T(8,128)(2,1)} %collective-permute-done.2, ...), kind=kLoop, calls=%fused_computation.331 | loop fusion | flops 59470464 | bytes 5251584 | tf_op jit(solution)/shard_map/reduce_sum | solution.py:57
  386.2 17.8 %fusion.129 = (f32[384]{0:T(512)S(1)}, f32[384]{0:T(512)S(1)}, f32[384]{0:T(512)S(1)}, f32[384]{0:T(512)S(1)}, f32[384]{0:T(512)S(1)}, /*index=5*/f32[384]{0:T(5...) fusion(bf16[16,176,384]{2,1,0:T(8,128)(2,1)S(1)} %bitcast.89, bf16[22,182,192]{2,1,0:T(8,128)(2,1)} %collective-permute-done.2, ...), kind=kLoop, calls=%fused_computation.334 | loop fusion | flops 59470464 | bytes 5251584 | tf_op jit(solution)/shard_map/reduce_sum | solution.py:57
  404.1 17.4 %fusion.128 = (f32[384]{0:T(512)S(1)}, f32[384]{0:T(512)S(1)}, f32[384]{0:T(512)S(1)}, f32[384]{0:T(512)S(1)}, f32[384]{0:T(512)S(1)}, /*index=5*/f32[384]{0:T(5...) fusion(bf16[16,176,384]{2,1,0:T(8,128)(2,1)S(1)} %bitcast.90, bf16[22,182,192]{2,1,0:T(8,128)(2,1)} %collective-permute-done.2, ...), kind=kLoop, calls=%fused_computation.333 | loop fusion | flops 59470464 | bytes 5251584 | tf_op jit(solution)/shard_map/reduce_sum | solution.py:57
  421.5 17.3 %fusion.127 = (f32[384]{0:T(512)S(1)}, f32[384]{0:T(512)S(1)}, f32[384]{0:T(512)S(1)}, f32[384]{0:T(512)S(1)}, f32[384]{0:T(512)S(1)}, /*index=5*/f32[384]{0:T(5...) fusion(bf16[16,176,384]{2,1,0:T(8,128)(2,1)S(1)} %bitcast.91, bf16[22,182,192]{2,1,0:T(8,128)(2,1)} %collective-permute-done.2, ...), kind=kLoop, calls=%fused_computation.332 | loop fusion | flops 59470464 | bytes 5251584 | tf_op jit(solution)/shard_map/reduce_sum | solution.py:57
  441.4 4.7 collective-permute-start.6
  452.8 7.5 %reshape.698 = bf16[16,11,16,2,192]{4,3,2,1,0:T(2,128)(2,1)} reshape(bf16[2816,384]{1,0:T(8,128)(2,1)} %get-tuple-element.185) | data formatting | bytes 4325376 | tf_op jit(solution)/shard_map/reshape | solution.py:146
  464.3 5.8 reshape.699
  470.0 4.2 gather_fusion.1
  478.2 6.9 all-to-all-start
  487.0 6.3 maximum_maximum_fusion
  498.2 57.5 %select_convert_fusion = bf16[16,176,384]{2,1,0:T(8,128)(2,1)S(1)} fusion(bf16[16,176,384]{2,1,0:T(8,128)(2,1)} %bitcast.94, bf16[3,176,384]{2,1,0:T(8,128)(2,1)S(1)} %collective-permute-done.7, bf16[3,176,384]{2,1,0:T(8,128)(2,1)} %copy-done.16, bf16[22,179,384]{2,1,0:T(8,128)(2,1)} %get-tuple-element.189, ...), kind=kLoop, calls=%fused_computation.341 | loop fusion | flops 166526976 | bytes 96044720 | tf_op jit(solution)/shard_map/convert_element_type | solution.py:200
  566.4 115.0 %all-reduce.4.cloned.1.call-done = (f32[175104]{0:T(1024)}, f32[384,768]{1,0:T(8,128)}, f32[768,384]{0,1:T(8,128)}) async-done(((f32[175104]{0:T(1024)}, f32[384,768]{1,0:T(8,128)}, f32[768,384]{0,1:T(8,128)}), (f32[175104]{0:T(1024)}, f32[384,768]{1,0:T(8,128)}, f32[768,384]{0,1:T(8,128)})) %all-reduce.4.cloned.1.call-update) | async-done | bytes 3059728
  (396 shorter events, 100.2 us)
Async XLA Ops:
  9.0 116.2 %collective-permute-start.3 = (f32[10944]{0:T(1024)S(1)}, f32[10944]{0:T(1024)S(1)}, u32[]{:S(2)}, u32[]{:S(2)}) collective-permute-start(f32[10944]{0:T(1024)S(1)} %concatenate.132), channel_id=1, source_target_pairs={{0,1},{1,0},{2,3},{3,2},{4,5},{5,4},{6,7},{7,6},{8,9},{9,8},{10,11... | collective-permute-start | bytes 131336 | tf_op jit(solution)/shard_map/ppermute | solution.py:17
  11.7 120.6 %collective-permute-start.5 = (bf16[768,384]{0,1:T(8,128)(2,1)}, bf16[768,384]{0,1:T(8,128)(2,1)}, u32[]{:S(2)}, u32[]{:S(2)}) collective-permute-start(bf16[768,384]{0,1:T(8,128)(2,1)} %copy.101), channel_id=1, source_target_pairs={{0,1},{1,0},{2,3},{3,2},{4,5},{5,4},{6,7},{7,6},{8,9},{9,8},{10,11... | collective-permute-start | bytes 1769480 | tf_op jit(solution)/shard_map/ppermute | solution.py:17
  11.7 119.4 %collective-permute-start.4 = (bf16[384,768]{1,0:T(8,128)(2,1)}, bf16[384,768]{1,0:T(8,128)(2,1)}, u32[]{:S(2)}, u32[]{:S(2)}) collective-permute-start(bf16[384,768]{1,0:T(8,128)(2,1)} %param.17), channel_id=1, source_target_pairs={{0,1},{1,0},{2,3},{3,2},{4,5},{5,4},{6,7},{7,6},{8,9},{9,8},{10,11... | collective-permute-start | bytes 1769480 | tf_op jit(solution)/shard_map/ppermute | solution.py:17
  21.3 77.6 %collective-permute-start.1 = (bf16[3,352,192]{1,2,0:T(8,128)(2,1)S(1)}, bf16[3,352,192]{1,2,0:T(8,128)(2,1)}, u32[]{:S(2)}, u32[]{:S(2)}) collective-permute-start(bf16[3,352,192]{1,2,0:T(8,128)(2,1)S(1)} %copy.97), channel_id=1, source_target_pairs={{2,0},{4,2},{6,4},{8,6},{10,8},{12,10},{14,12},{16,14},{18,16},{20... | collective-permute-start | bytes 1216520 | tf_op jit(solution)/shard_map/ppermute | solution.py:25
  23.6 76.5 %collective-permute-start = (bf16[3,352,192]{1,2,0:T(8,128)(2,1)}, bf16[3,352,192]{1,2,0:T(8,128)(2,1)}, u32[]{:S(2)}, u32[]{:S(2)}) collective-permute-start(bf16[3,352,192]{1,2,0:T(8,128)(2,1)} %copy.96), channel_id=1, source_target_pairs={{0,2},{2,4},{4,6},{6,8},{8,10},{10,12},{12,14},{14,16},{16,18},{18... | collective-permute-start | bytes 1216520 | tf_op jit(solution)/shard_map/ppermute | solution.py:24
  89.5 168.9 %all-to-all-start.1 = ((bf16[32,16,3072]{2,1,0:T(8,128)(2,1)}), bf16[32,16,3072]{2,1,0:T(8,128)(2,1)}, u32[]{:S(2)}, u32[]{:S(2)}) async-start(bf16[32,16,3072]{2,1,0:T(8,128)(2,1)} %broadcast_select_fusion.1), calls=%async_computation.1 | async-start | bytes 6291456 | tf_op jit(solution)/shard_map/all_to_all | solution.py:100
  121.5 115.6 %copy-start.5 = (bf16[22,182,192]{2,1,0:T(8,128)(2,1)}, bf16[22,182,192]{2,1,0:T(8,128)(2,1)S(1)}, u32[]{:S(2)}) copy-start(bf16[22,182,192]{2,1,0:T(8,128)(2,1)S(1)} %get-tuple-element.187) | copy-start | bytes 4612612
  121.5 14.6 %collective-permute-start.2 = (bf16[22,182,192]{2,1,0:T(8,128)(2,1)}, bf16[22,182,192]{2,1,0:T(8,128)(2,1)}, u32[]{:S(2)}, u32[]{:S(2)}) collective-permute-start(bf16[22,182,192]{2,1,0:T(8,128)(2,1)} %get-tuple-element.186), channel_id=1, source_target_pairs={{0,1},{1,0},{2,3},{3,2},{4,5},{5,4},{6,7},{7,6},{8,9},{9,8},{10,11... | collective-permute-start | bytes 4612616 | tf_op jit(solution)/shard_map/ppermute | solution.py:17
  127.6 108.9 %copy-start.29 = (f32[384]{0:T(512)}, f32[384]{0:T(512)S(1)}, u32[]{:S(2)}) copy-start(f32[384]{0:T(512)S(1)} %get-tuple-element.167) | copy-start | bytes 4612
  127.6 108.9 %copy-start.30 = (f32[384]{0:T(512)}, f32[384]{0:T(512)S(1)}, u32[]{:S(2)}) copy-start(f32[384]{0:T(512)S(1)} %get-tuple-element.168) | copy-start | bytes 4612
  127.6 108.9 %copy-start.31 = (f32[384]{0:T(512)}, f32[384]{0:T(512)S(1)}, u32[]{:S(2)}) copy-start(f32[384]{0:T(512)S(1)} %get-tuple-element.169) | copy-start | bytes 4612
  127.8 108.7 %copy-start.32 = (f32[384]{0:T(512)}, f32[384]{0:T(512)S(1)}, u32[]{:S(2)}) copy-start(f32[384]{0:T(512)S(1)} %get-tuple-element.152) | copy-start | bytes 4612
  127.8 108.7 %copy-start.33 = (f32[384]{0:T(512)}, f32[384]{0:T(512)S(1)}, u32[]{:S(2)}) copy-start(f32[384]{0:T(512)S(1)} %get-tuple-element.153) | copy-start | bytes 4612
  127.8 108.7 %copy-start.34 = (f32[384]{0:T(512)}, f32[384]{0:T(512)S(1)}, u32[]{:S(2)}) copy-start(f32[384]{0:T(512)S(1)} %get-tuple-element.154) | copy-start | bytes 4612
  127.8 108.7 %copy-start.35 = (f32[384]{0:T(512)}, f32[384]{0:T(512)S(1)}, u32[]{:S(2)}) copy-start(f32[384]{0:T(512)S(1)} %get-tuple-element.155) | copy-start | bytes 4612
  127.8 108.7 %copy-start.36 = (f32[384]{0:T(512)}, f32[384]{0:T(512)S(1)}, u32[]{:S(2)}) copy-start(f32[384]{0:T(512)S(1)} %get-tuple-element.156) | copy-start | bytes 4612
  127.8 108.7 %copy-start.37 = (f32[384]{0:T(512)}, f32[384]{0:T(512)S(1)}, u32[]{:S(2)}) copy-start(f32[384]{0:T(512)S(1)} %get-tuple-element.157) | copy-start | bytes 4612
  127.8 108.7 %copy-start.38 = (f32[384]{0:T(512)}, f32[384]{0:T(512)S(1)}, u32[]{:S(2)}) copy-start(f32[384]{0:T(512)S(1)} %get-tuple-element.158) | copy-start | bytes 4612
  127.8 108.7 %copy-start.39 = (f32[384]{0:T(512)}, f32[384]{0:T(512)S(1)}, u32[]{:S(2)}) copy-start(f32[384]{0:T(512)S(1)} %get-tuple-element.159) | copy-start | bytes 4612
  127.8 108.7 %copy-start.40 = (f32[384]{0:T(512)}, f32[384]{0:T(512)S(1)}, u32[]{:S(2)}) copy-start(f32[384]{0:T(512)S(1)} %get-tuple-element.160) | copy-start | bytes 4612
  129.8 112.1 %copy-start.68 = (f32[384]{0:T(512)}, f32[384]{0:T(512)S(1)}, u32[]{:S(2)}) copy-start(f32[384]{0:T(512)S(1)} %get-tuple-element.229) | copy-start | bytes 4612
  132.2 111.3 %copy-start.20 = (bf16[384,1536]{1,0:T(8,128)(2,1)}, bf16[384,1536]{1,0:T(8,128)(2,1)S(1)}, u32[]{:S(2)}) copy-start(bf16[384,1536]{1,0:T(8,128)(2,1)S(1)} %constant_dynamic-update-slice_fusion) | copy-start | bytes 3538948
  342.3 142.9 %copy-start.4 = (bf16[2816,384]{1,0:T(8,128)(2,1)}, bf16[2816,384]{1,0:T(8,128)(2,1)S(1)}, u32[]{:S(2)}) copy-start(bf16[2816,384]{1,0:T(8,128)(2,1)S(1)} %multiply_convert_fusion.1) | copy-start | bytes 6488068
  439.6 46.0 %collective-permute-start.10 = (f32[10944]{0:T(1024)S(1)}, f32[10944]{0:T(1024)S(1)}, u32[]{:S(2)}, u32[]{:S(2)}) collective-permute-start(f32[10944]{0:T(1024)S(1)} %pad_maximum_fusion.9), channel_id=1, source_target_pairs={{0,1},{1,0},{2,3},{3,2},{4,5},{5,4},{6,7},{7,6},{8,9},{9,8},{10,11... | collective-permute-start | bytes 131336 | tf_op jit(solution)/shard_map/ppermute | solution.py:17
  440.0 45.2 %collective-permute-start.7 = (bf16[3,176,384]{2,1,0:T(8,128)(2,1)}, bf16[3,176,384]{2,1,0:T(8,128)(2,1)S(1)}, u32[]{:S(2)}, u32[]{:S(2)}) collective-permute-start(bf16[3,176,384]{2,1,0:T(8,128)(2,1)} %bitcast.110), channel_id=1, source_target_pairs={{2,0},{4,2},{6,4},{8,6},{10,8},{12,10},{14,12},{16,14},{18,16},{20... | collective-permute-start | bytes 1216520 | tf_op jit(solution)/shard_map/ppermute | solution.py:25
  441.4 43.8 %collective-permute-start.6 = (bf16[3,176,384]{2,1,0:T(8,128)(2,1)S(1)}, bf16[3,176,384]{2,1,0:T(8,128)(2,1)S(1)}, u32[]{:S(2)}, u32[]{:S(2)}) collective-permute-start(bf16[3,176,384]{2,1,0:T(8,128)(2,1)S(1)} %bitcast.109), channel_id=1, source_target_pairs={{0,2},{2,4},{4,6},{6,8},{8,10},{10,12},{12,14},{14,16},{16,18},{18... | collective-permute-start | bytes 1216520 | tf_op jit(solution)/shard_map/ppermute | solution.py:24
  449.4 43.8 %collective-permute-start.11 = (f32[384,768]{1,0:T(8,128)}, f32[384,768]{1,0:T(8,128)}, u32[]{:S(2)}, u32[]{:S(2)}) collective-permute-start(f32[384,768]{1,0:T(8,128)} %slice.1161), channel_id=1, source_target_pairs={{0,1},{1,0},{2,3},{3,2},{4,5},{5,4},{6,7},{7,6},{8,9},{9,8},{10,11... | collective-permute-start | bytes 3538952 | tf_op jit(solution)/shard_map/ppermute | solution.py:17
  452.8 43.0 %collective-permute-start.12 = (f32[768,384]{0,1:T(8,128)}, f32[768,384]{0,1:T(8,128)}, u32[]{:S(2)}, u32[]{:S(2)}) collective-permute-start(f32[768,384]{0,1:T(8,128)} %slice.1166), channel_id=1, source_target_pairs={{0,1},{1,0},{2,3},{3,2},{4,5},{5,4},{6,7},{7,6},{8,9},{9,8},{10,11... | collective-permute-start | bytes 3538952 | tf_op jit(solution)/shard_map/ppermute | solution.py:17
  478.2 209.4 %all-to-all-start = ((bf16[32,16,3072]{2,1,0:T(8,128)(2,1)}), bf16[32,16,3072]{2,1,0:T(8,128)(2,1)}, u32[]{:S(2)}, u32[]{:S(2)}) async-start(bf16[32,16,3072]{2,1,0:T(8,128)(2,1)} %broadcast_select_fusion.2), calls=%async_computation | async-start | bytes 6291456 | tf_op jit(solution)/shard_map/all_to_all | solution.py:155
  485.1 196.2 %all-reduce.4.cloned.1.call-start = ((), (), s32[]{:S(2)}) async-start(), calls=%async_computation.2 | async-start | bytes 6119424
  485.3 1.4 collective-permute-start.8
  557.5 3.4 collective-permute-start.9
  (78 other events, 3106.0 us)
Sparse Core Ops, SparseCore 0:
  498.4 182.9 all-reduce.3
